TPU v7x, 32 devices: a whole 2x2x4 slice. The times are simulated.
32 devices in a mesh: ctx: 4 (over y, core), ch: 8 (over z, x).
Axes of the slice: x: 2, y: 2, z: 4, core: 2. Of those that a mesh axis runs over, the one named last changes fastest.
Arguments:
- query: bfloat16 [128, 4096], P('ch', 'ctx'), may hold values from -16 to 16
- key_branch: bfloat16 [128, 4096], P('ch', 'ctx'), may hold values from -6 to 6
- value_branch: bfloat16 [128, 4096], P('ch', 'ctx'), may hold values from -6 to 6
- residue: float32 [128, 16], P('ch'), may hold values from -1.5 to 1.5
- rate: float32 [128, 16], P('ch'), may hold values from 6.1035156e-05 to 0.03
- skip: float32 [128], P('ch'), may hold values from -4 to 4
- gain: float32 [128], P('ch'), may hold values from 0.1 to 1.9
Outputs:
- mixed_out: bfloat16 [128, 4096], P('ch', 'ctx')
All inputs are finite; a program needn't handle non-finite values.
Results may differ from a plain program's by a relative error of at most 0.009.
Values may be sent and summed in bfloat16 or wider, within the bound.
A program may use at most 64 MiB of HBM per device.

v0:
```python
import functools

import jax
import jax.numpy as jnp
from jax import lax
from jax.experimental import pallas as pl
from jax.experimental.pallas import tpu as pltpu
from jax.sharding import PartitionSpec as P

F32 = jnp.float32
BF16 = jnp.bfloat16
MESH = pl.DeviceIdType.MESH
CHUNK = 128


def split(value):
    high = value.astype(BF16)
    return high, (value - high.astype(F32)).astype(BF16)


def dot(left, right):
    return jnp.dot(left, right, preferred_element_type=F32)


def dot_nt(left, right):
    return lax.dot_general(left, right, (((1,), (1,)), ((), ())), preferred_element_type=F32)


def one_minus_exp(x):
    series = jnp.ones_like(x)
    for order in range(10, 1, -1):
        series = 1.0 - x * (1.0 / order) * series
    return jnp.where(x < 0.25, x * series, 1.0 - jnp.exp(-x))


def column(row, rows):
    width = row.shape[1]
    keep = lax.broadcasted_iota(jnp.int32, (rows, width), 0) == lax.broadcasted_iota(
        jnp.int32, (rows, width), 1
    )
    return jnp.sum(jnp.where(keep, row, 0.0), axis=1, keepdims=True)


def kernel(
    n_ctx, n_ch, query_hbm, key_hbm, value_hbm, residue_hbm, rate_hbm, skip_hbm, gain_hbm, out_ref,
    query_ref, key_ref, value_ref, residue_ref, rate_ref, skip_ref, gain_ref,
    toeplitz, spread, state, state_slots, square, square_slots,
    in_sems, state_send, state_recv, square_send, square_recv,
):
    my_ctx, my_ch = lax.axis_index("ctx"), lax.axis_index("ch")
    channels, block = query_ref.shape
    modes = rate_ref.shape[1]
    width = channels * modes
    chunks = block // CHUNK

    loads = [
        pltpu.make_async_copy(src, dst, in_sems.at[i])
        for i, (src, dst) in enumerate(
            (
                (rate_hbm, rate_ref), (residue_hbm, residue_ref), (key_hbm, key_ref),
                (value_hbm, value_ref), (skip_hbm, skip_ref), (gain_hbm, gain_ref),
                (query_hbm, query_ref),
            )
        )
    ]
    for load in loads:
        load.start()

    barrier = pltpu.get_barrier_semaphore()
    for step in range(1, n_ctx):
        pl.semaphore_signal(
            barrier, inc=1, device_id={"ctx": lax.rem(my_ctx + step, n_ctx)}, device_id_type=MESH
        )
    for step in range(1, n_ch):
        pl.semaphore_signal(
            barrier, inc=1, device_id={"ch": lax.rem(my_ch + step, n_ch)}, device_id_type=MESH
        )

    loads[0].wait()
    loads[1].wait()
    lane = lax.broadcasted_iota(jnp.int32, (channels, width), 1)
    own = lane // modes == lax.broadcasted_iota(jnp.int32, (channels, width), 0)
    mode_lane = lax.broadcasted_iota(jnp.int32, (modes, width), 1)
    mode_row = lax.broadcasted_iota(jnp.int32, (modes, width), 0)
    pick = (lax.rem(mode_lane, modes) == mode_row).astype(F32)
    tiled = jnp.dot(
        jnp.concatenate([rate_ref[...], residue_ref[...]], axis=0), pick,
        precision=lax.Precision.HIGHEST, preferred_element_type=F32,
    )
    rate_tiled, residue_tiled = tiled[:channels], tiled[channels:]
    rate_row = jnp.sum(jnp.where(own, rate_tiled, 0.0), axis=0, keepdims=True)
    place = lax.broadcasted_iota(jnp.int32, (CHUNK, width), 0).astype(F32)
    tail_high, tail_low = split(jnp.exp(-rate_row * (CHUNK - place)))
    chunk_decay = jnp.exp(-rate_row * float(CHUNK))

    loads[2].wait()
    loads[3].wait()
    pieces = [
        key_ref[:, k * CHUNK:(k + 1) * CHUNK] * value_ref[:, k * CHUNK:(k + 1) * CHUNK]
        for k in range(chunks)
    ]
    signal = jnp.concatenate(pieces, axis=0)
    update = dot(signal, tail_high) + dot(signal, tail_low)
    held = jnp.zeros((channels, width), F32)
    states = []
    for k in range(chunks):
        states.append(held)
        held = chunk_decay * held + update[k * channels:(k + 1) * channels]
    state[...] = jnp.sum(jnp.where(own, held, 0.0), axis=0, keepdims=True)

    pl.semaphore_wait(barrier, n_ctx + n_ch - 2)
    state_copies = [
        pltpu.make_async_remote_copy(
            src_ref=state, dst_ref=state_slots.at[step - 1],
            send_sem=state_send.at[step - 1], recv_sem=state_recv.at[step - 1],
            device_id={"ctx": lax.rem(my_ctx + step, n_ctx)}, device_id_type=MESH,
        )
        for step in range(1, n_ctx)
    ]
    for copy in state_copies:
        copy.start()

    head_high, head_low = split(jnp.exp(-rate_row * place))
    scaled = jnp.where(own, jnp.sqrt(one_minus_exp(2.0 * rate_tiled)) * residue_tiled, 0.0)
    scaled_high, scaled_low = split(scaled)
    taps = (
        dot_nt(scaled_high, head_high) + dot_nt(scaled_high, head_low)
        + dot_nt(scaled_low, head_high)
    )
    loads[4].wait()
    loads[5].wait()
    first = lax.broadcasted_iota(jnp.int32, (channels, CHUNK), 1) == 0
    taps = taps + jnp.where(first, column(skip_ref[...], channels), 0.0)
    gain = column(gain_ref[...], channels)
    causal = lax.broadcasted_iota(jnp.int32, (CHUNK, CHUNK), 1) >= lax.broadcasted_iota(
        jnp.int32, (CHUNK, CHUNK), 0
    )
    rows = lax.broadcasted_iota(jnp.int32, (channels, CHUNK), 0)
    for c in range(channels):
        rolled = pltpu.roll(
            jnp.broadcast_to(taps[c:c + 1], (CHUNK, CHUNK)), 0, 1, stride=1, stride_axis=0
        )
        toeplitz[c * CHUNK:(c + 1) * CHUNK, :] = jnp.where(causal, rolled, 0.0).astype(BF16)
        this = (rows == c).astype(F32).astype(BF16)
        for k in range(chunks):
            spread[k * channels:(k + 1) * channels, c * CHUNK:(c + 1) * CHUNK] = pieces[k] * this
    near = dot(spread[...], toeplitz[...])
    loads[6].wait()

    carry = jnp.zeros((1, width), F32)
    for step in range(1, n_ctx):
        state_copies[step - 1].wait_recv()
        weight = (my_ctx >= step).astype(F32)
        carry = carry + weight * jnp.exp(-rate_row * float(block * (step - 1))) * state_slots[step - 1]
    full = jnp.concatenate(
        [
            (states[k] + jnp.exp(-rate_row * float(CHUNK * k)) * carry) * scaled
            for k in range(chunks)
        ],
        axis=0,
    )
    full_high, full_low = split(full)
    conv = near + (
        dot_nt(full_high, head_high) + dot_nt(full_high, head_low) + dot_nt(full_low, head_high)
    )
    mixed = []
    for k in range(chunks):
        part = query_ref[:, k * CHUNK:(k + 1) * CHUNK].astype(F32) * conv[k * channels:(k + 1) * channels]
        mixed.append(part)
        square[k:k + 1, :] = jnp.sum(part * part, axis=0, keepdims=True)

    square_copies = [
        pltpu.make_async_remote_copy(
            src_ref=square, dst_ref=square_slots.at[step - 1],
            send_sem=square_send.at[step - 1], recv_sem=square_recv.at[step - 1],
            device_id={"ch": lax.rem(my_ch + step, n_ch)}, device_id_type=MESH,
        )
        for step in range(1, n_ch)
    ]
    for copy in square_copies:
        copy.start()
    total = square[...]
    for step in range(1, n_ch):
        square_copies[step - 1].wait_recv()
        total = total + square_slots[step - 1]
    scale = lax.rsqrt(total * (1.0 / (channels * n_ch)) + 1e-06)
    for k in range(chunks):
        out_ref[:, k * CHUNK:(k + 1) * CHUNK] = (mixed[k] * scale[k:k + 1] * gain).astype(BF16)
    for copy in state_copies + square_copies:
        copy.wait_send()


def body(mesh_shape, query, key_branch, value_branch, residue, rate, skip, gain):
    n_ctx, n_ch = mesh_shape
    channels, block = query.shape
    modes = rate.shape[1]
    width = channels * modes
    chunks = block // CHUNK
    arrays = tuple(pltpu.with_memory_space_constraint(a, pltpu.HBM) for a in (
        query, key_branch, value_branch, residue, rate,
        skip.reshape(1, channels), gain.reshape(1, channels),
    ))
    return pl.pallas_call(
        functools.partial(kernel, n_ctx, n_ch),
        out_shape=pltpu.VMEM((channels, block), BF16),
        in_specs=[pl.BlockSpec(memory_space=pltpu.HBM)] * len(arrays),
        out_specs=pl.BlockSpec(memory_space=pltpu.VMEM),
        scratch_shapes=[pltpu.VMEM(a.shape, a.dtype) for a in arrays] + [
            pltpu.VMEM((channels * CHUNK, CHUNK), BF16),
            pltpu.VMEM((chunks * channels, channels * CHUNK), BF16),
            pltpu.VMEM((1, width), F32),
            pltpu.VMEM((n_ctx - 1, 1, width), F32),
            pltpu.VMEM((chunks, CHUNK), F32),
            pltpu.VMEM((n_ch - 1, chunks, CHUNK), F32),
            pltpu.SemaphoreType.DMA((len(arrays),)),
            pltpu.SemaphoreType.DMA((n_ctx - 1,)),
            pltpu.SemaphoreType.DMA((n_ctx - 1,)),
            pltpu.SemaphoreType.DMA((n_ch - 1,)),
            pltpu.SemaphoreType.DMA((n_ch - 1,)),
        ],
        compiler_params=pltpu.CompilerParams(
            collective_id=0, has_side_effects=True
        ),
        cost_estimate=pl.CostEstimate(flops=150_000_000, bytes_accessed=140_000, transcendentals=80_000),
    )(*arrays)


def solution(mesh):
    placed = (
        P("ch", "ctx"), P("ch", "ctx"), P("ch", "ctx"), P("ch", None), P("ch", None), P("ch"), P("ch"),
    )
    sizes = (mesh.shape["ctx"], mesh.shape["ch"])
    return jax.shard_map(
        functools.partial(body, sizes), mesh=mesh, in_specs=placed, out_specs=P("ch", "ctx"),
        check_vma=False,
    )
```

profile of v0, /device:TPU:0, one launch (start us, length us, event | category | flops | bytes accessed | tf_op | source)
XLA Modules:
  0.0 13.1 jit_solution(219061337307847096)
XLA Ops:
  0.0 12.5 %shard_map.73 = bf16[16,1024]{1,0:T(8,128)(2,1)S(1)} custom-call(bf16[16,1024]{1,0:T(8,128)(2,1)} %query_hbm.1, bf16[16,1024]{1,0:T(8,128)(2,1)} %key_hbm.1, bf16[16,1024]{1,0:T(8,128)(2,1)} %value_hbm.1, f32[16,16]{1,0:T(8,128)} %residue_hbm.1, f32[16,16]{1,0:T(8,128)} %rate_hbm.1, f32[1,16]{1,0:T(1,128)} %bitcast.2, f32[1,16]{1,0:T(1,128)} %bitcast.3), custom_call_target="tpu_custom_call" | custom-call | flops 150000000 | bytes 140000 | tf_op jit(solution)/shard_map/pallas_call | solution.py:203
  12.5 0.6 %copy.9 = bf16[16,1024]{1,0:T(8,128)(2,1)} copy(bf16[16,1024]{1,0:T(8,128)(2,1)S(1)} %shard_map.73) | data formatting | bytes 65536
where the time goes:
time: 13.3 us; the launch traced here: 13.1 us
  Pallas kernels  12.5 us (94%)
  local copies, waits for them, and re-layouts  0.62 us (5%)
    pallas_call x1, Pallas kernels, body(): pl.pallas_call(functools.partial(kernel, n_ctx, n_ch), out_shape=pltpu.VM...  12.5 us
    unnamed x1, local copies, waits for them, and re-layouts  0.62 us

commit v1 on v0

--- a/solution.py
+++ b/solution.py
@@ -63,31 +63,29 @@
             )
         )
     ]
-    for load in loads:
-        load.start()
-
+    loads[0].start()
     barrier = pltpu.get_barrier_semaphore()
     for step in range(1, n_ctx):
-        pl.semaphore_signal(
-            barrier, inc=1, device_id={"ctx": lax.rem(my_ctx + step, n_ctx)}, device_id_type=MESH
-        )
+        @pl.when(my_ctx >= step)
+        def greet():
+            pl.semaphore_signal(
+                barrier, inc=1, device_id={"ctx": my_ctx - step}, device_id_type=MESH
+            )
+
+        @pl.when(my_ctx < step)
+        def clear():
+            state_slots[step - 1] = jnp.zeros((1, width), F32)
     for step in range(1, n_ch):
         pl.semaphore_signal(
             barrier, inc=1, device_id={"ch": lax.rem(my_ch + step, n_ch)}, device_id_type=MESH
         )
 
+    for load in loads[1:]:
+        load.start()
     loads[0].wait()
-    loads[1].wait()
     lane = lax.broadcasted_iota(jnp.int32, (channels, width), 1)
     own = lane // modes == lax.broadcasted_iota(jnp.int32, (channels, width), 0)
-    mode_lane = lax.broadcasted_iota(jnp.int32, (modes, width), 1)
-    mode_row = lax.broadcasted_iota(jnp.int32, (modes, width), 0)
-    pick = (lax.rem(mode_lane, modes) == mode_row).astype(F32)
-    tiled = jnp.dot(
-        jnp.concatenate([rate_ref[...], residue_ref[...]], axis=0), pick,
-        precision=lax.Precision.HIGHEST, preferred_element_type=F32,
-    )
-    rate_tiled, residue_tiled = tiled[:channels], tiled[channels:]
+    rate_tiled = jnp.concatenate([rate_ref[...]] * channels, axis=1)
     rate_row = jnp.sum(jnp.where(own, rate_tiled, 0.0), axis=0, keepdims=True)
     place = lax.broadcasted_iota(jnp.int32, (CHUNK, width), 0).astype(F32)
     tail_high, tail_low = split(jnp.exp(-rate_row * (CHUNK - place)))
@@ -108,7 +106,7 @@
         held = chunk_decay * held + update[k * channels:(k + 1) * channels]
     state[...] = jnp.sum(jnp.where(own, held, 0.0), axis=0, keepdims=True)
 
-    pl.semaphore_wait(barrier, n_ctx + n_ch - 2)
+    pl.semaphore_wait(barrier, n_ctx - 1 - my_ctx + n_ch - 1)
     state_copies = [
         pltpu.make_async_remote_copy(
             src_ref=state, dst_ref=state_slots.at[step - 1],
@@ -117,9 +115,11 @@
         )
         for step in range(1, n_ctx)
     ]
-    for copy in state_copies:
-        copy.start()
-
+    for step in range(1, n_ctx):
+        pl.when(my_ctx + step < n_ctx)(state_copies[step - 1].start)
+
+    loads[1].wait()
+    residue_tiled = jnp.concatenate([residue_ref[...]] * channels, axis=1)
     head_high, head_low = split(jnp.exp(-rate_row * place))
     scaled = jnp.where(own, jnp.sqrt(one_minus_exp(2.0 * rate_tiled)) * residue_tiled, 0.0)
     scaled_high, scaled_low = split(scaled)
@@ -149,9 +149,8 @@
 
     carry = jnp.zeros((1, width), F32)
     for step in range(1, n_ctx):
-        state_copies[step - 1].wait_recv()
-        weight = (my_ctx >= step).astype(F32)
-        carry = carry + weight * jnp.exp(-rate_row * float(block * (step - 1))) * state_slots[step - 1]
+        pl.when(my_ctx >= step)(state_copies[step - 1].wait_recv)
+        carry = carry + jnp.exp(-rate_row * float(block * (step - 1))) * state_slots[step - 1]
     full = jnp.concatenate(
         [
             (states[k] + jnp.exp(-rate_row * float(CHUNK * k)) * carry) * scaled
@@ -186,7 +185,9 @@
     scale = lax.rsqrt(total * (1.0 / (channels * n_ch)) + 1e-06)
     for k in range(chunks):
         out_ref[:, k * CHUNK:(k + 1) * CHUNK] = (mixed[k] * scale[k:k + 1] * gain).astype(BF16)
-    for copy in state_copies + square_copies:
+    for step in range(1, n_ctx):
+        pl.when(my_ctx + step < n_ctx)(state_copies[step - 1].wait_send)
+    for copy in square_copies:
         copy.wait_send()
 
 

time: 13.3 us -> 11.3 us (0.85)
  Pallas kernels: 12.5 us -> 10.5 us
    pallas_call x1, Pallas kernels: 12.5 us -> 10.5 us  [body(): pl.pallas_call(functools.partial(kernel, n_ctx, n_ch), out_shape=pltpu.VM...]
where the time goes in v1:
time: 11.3 us; the launch traced here: 11.1 us
  Pallas kernels  10.5 us (93%)
  local copies, waits for them, and re-layouts  0.62 us (5%)
    pallas_call x1, Pallas kernels, body(): pl.pallas_call(functools.partial(kernel, n_ctx, n_ch), out_shape=pltpu.VM...  10.5 us
    unnamed x1, local copies, waits for them, and re-layouts  0.62 us

profile of v1, /device:TPU:0, one launch (start us, length us, event | category | flops | bytes accessed | tf_op | source)
XLA Modules:
  0.0 11.1 jit_solution(15438121145086671688)
XLA Ops:
  0.0 10.5 %shard_map.73 = bf16[16,1024]{1,0:T(8,128)(2,1)S(1)} custom-call(bf16[16,1024]{1,0:T(8,128)(2,1)} %query_hbm.1, bf16[16,1024]{1,0:T(8,128)(2,1)} %key_hbm.1, bf16[16,1024]{1,0:T(8,128)(2,1)} %value_hbm.1, f32[16,16]{1,0:T(8,128)} %residue_hbm.1, f32[16,16]{1,0:T(8,128)} %rate_hbm.1, f32[1,16]{1,0:T(1,128)} %bitcast.2, f32[1,16]{1,0:T(1,128)} %bitcast.3), custom_call_target="tpu_custom_call" | custom-call | flops 150000000 | bytes 140000 | tf_op jit(solution)/shard_map/pallas_call | solution.py:204
  10.5 0.6 %copy.9 = bf16[16,1024]{1,0:T(8,128)(2,1)} copy(bf16[16,1024]{1,0:T(8,128)(2,1)S(1)} %shard_map.73) | data formatting | bytes 65536

commit v2 on v1

--- a/solution.py
+++ b/solution.py
@@ -63,7 +63,8 @@
             )
         )
     ]
-    loads[0].start()
+    for i in (0, 2, 3):
+        loads[i].start()
     barrier = pltpu.get_barrier_semaphore()
     for step in range(1, n_ctx):
         @pl.when(my_ctx >= step)
@@ -80,15 +81,20 @@
             barrier, inc=1, device_id={"ch": lax.rem(my_ch + step, n_ch)}, device_id_type=MESH
         )
 
-    for load in loads[1:]:
-        load.start()
+    for i in (1, 4, 5, 6):
+        loads[i].start()
     loads[0].wait()
     lane = lax.broadcasted_iota(jnp.int32, (channels, width), 1)
     own = lane // modes == lax.broadcasted_iota(jnp.int32, (channels, width), 0)
     rate_tiled = jnp.concatenate([rate_ref[...]] * channels, axis=1)
     rate_row = jnp.sum(jnp.where(own, rate_tiled, 0.0), axis=0, keepdims=True)
-    place = lax.broadcasted_iota(jnp.int32, (CHUNK, width), 0).astype(F32)
-    tail_high, tail_low = split(jnp.exp(-rate_row * (CHUNK - place)))
+    fine = lax.broadcasted_iota(jnp.int32, (8, width), 0).astype(F32)
+    coarse = 8.0 * lax.broadcasted_iota(jnp.int32, (CHUNK // 8, width), 0).astype(F32)
+    tail_fine = jnp.exp(-rate_row * (8.0 - fine))
+    powers = jnp.exp(-rate_row * coarse)
+    tail_high, tail_low = split(
+        jnp.concatenate([tail_fine * powers[i:i + 1] for i in reversed(range(CHUNK // 8))], axis=0)
+    )
     chunk_decay = jnp.exp(-rate_row * float(CHUNK))
 
     loads[2].wait()
@@ -106,6 +112,18 @@
         held = chunk_decay * held + update[k * channels:(k + 1) * channels]
     state[...] = jnp.sum(jnp.where(own, held, 0.0), axis=0, keepdims=True)
 
+    loads[1].wait()
+    residue_tiled = jnp.concatenate([residue_ref[...]] * channels, axis=1)
+    head_fine = jnp.exp(-rate_row * fine)
+    head_high, head_low = split(
+        jnp.concatenate([head_fine * powers[i:i + 1] for i in range(CHUNK // 8)], axis=0)
+    )
+    scaled = jnp.where(own, jnp.sqrt(one_minus_exp(2.0 * rate_tiled)) * residue_tiled, 0.0)
+    scaled_high, scaled_low = split(scaled)
+    taps = (
+        dot_nt(scaled_high, head_high) + dot_nt(scaled_high, head_low)
+        + dot_nt(scaled_low, head_high)
+    )
     pl.semaphore_wait(barrier, n_ctx - 1 - my_ctx + n_ch - 1)
     state_copies = [
         pltpu.make_async_remote_copy(
@@ -118,15 +136,6 @@
     for step in range(1, n_ctx):
         pl.when(my_ctx + step < n_ctx)(state_copies[step - 1].start)
 
-    loads[1].wait()
-    residue_tiled = jnp.concatenate([residue_ref[...]] * channels, axis=1)
-    head_high, head_low = split(jnp.exp(-rate_row * place))
-    scaled = jnp.where(own, jnp.sqrt(one_minus_exp(2.0 * rate_tiled)) * residue_tiled, 0.0)
-    scaled_high, scaled_low = split(scaled)
-    taps = (
-        dot_nt(scaled_high, head_high) + dot_nt(scaled_high, head_low)
-        + dot_nt(scaled_low, head_high)
-    )
     loads[4].wait()
     loads[5].wait()
     first = lax.broadcasted_iota(jnp.int32, (channels, CHUNK), 1) == 0
@@ -144,20 +153,17 @@
         this = (rows == c).astype(F32).astype(BF16)
         for k in range(chunks):
             spread[k * channels:(k + 1) * channels, c * CHUNK:(c + 1) * CHUNK] = pieces[k] * this
+    reach = [jnp.exp(-rate_row * float(CHUNK * k)) * scaled for k in range(chunks)]
+    ready = [states[k] * scaled for k in range(chunks)]
+    weights = [jnp.exp(-rate_row * float(block * step)) for step in range(n_ctx - 1)]
     near = dot(spread[...], toeplitz[...])
     loads[6].wait()
 
     carry = jnp.zeros((1, width), F32)
     for step in range(1, n_ctx):
         pl.when(my_ctx >= step)(state_copies[step - 1].wait_recv)
-        carry = carry + jnp.exp(-rate_row * float(block * (step - 1))) * state_slots[step - 1]
-    full = jnp.concatenate(
-        [
-            (states[k] + jnp.exp(-rate_row * float(CHUNK * k)) * carry) * scaled
-            for k in range(chunks)
-        ],
-        axis=0,
-    )
+        carry = carry + weights[step - 1] * state_slots[step - 1]
+    full = jnp.concatenate([ready[k] + reach[k] * carry for k in range(chunks)], axis=0)
     full_high, full_low = split(full)
     conv = near + (
         dot_nt(full_high, head_high) + dot_nt(full_high, head_low) + dot_nt(full_low, head_high)

time: 11.3 us -> 11.2 us (level)
  the two profiles are of different devices: /device:TPU:0 before, /device:TPU:4 now
where the time goes in v2:
time: 11.2 us; the launch traced here: 11 us
  Pallas kernels  10.4 us (93%)
  local copies, waits for them, and re-layouts  0.62 us (6%)
    pallas_call x1, Pallas kernels, body(): pl.pallas_call(functools.partial(kernel, n_ctx, n_ch), out_shape=pltpu.VM...  10.4 us
    unnamed x1, local copies, waits for them, and re-layouts  0.62 us

profile of v2, /device:TPU:4, one launch (start us, length us, event | category | flops | bytes accessed | tf_op | source)
XLA Modules:
  0.0 11.0 jit_solution(16550642617205899122)
XLA Ops:
  0.0 10.4 %shard_map.73 = bf16[16,1024]{1,0:T(8,128)(2,1)S(1)} custom-call(bf16[16,1024]{1,0:T(8,128)(2,1)} %query_hbm.1, bf16[16,1024]{1,0:T(8,128)(2,1)} %key_hbm.1, bf16[16,1024]{1,0:T(8,128)(2,1)} %value_hbm.1, f32[16,16]{1,0:T(8,128)} %residue_hbm.1, f32[16,16]{1,0:T(8,128)} %rate_hbm.1, f32[1,16]{1,0:T(1,128)} %bitcast.2, f32[1,16]{1,0:T(1,128)} %bitcast.3), custom_call_target="tpu_custom_call" | custom-call | flops 150000000 | bytes 140000 | tf_op jit(solution)/shard_map/pallas_call | solution.py:210
  10.4 0.6 %copy.9 = bf16[16,1024]{1,0:T(8,128)(2,1)} copy(bf16[16,1024]{1,0:T(8,128)(2,1)S(1)} %shard_map.73) | data formatting | bytes 65536

commit v3 on v2

--- a/solution.py
+++ b/solution.py
@@ -133,7 +133,7 @@
         )
         for step in range(1, n_ctx)
     ]
-    for step in range(1, n_ctx):
+    for step in reversed(range(1, n_ctx)):
         pl.when(my_ctx + step < n_ctx)(state_copies[step - 1].start)
 
     loads[4].wait()
@@ -182,7 +182,7 @@
         )
         for step in range(1, n_ch)
     ]
-    for copy in square_copies:
+    for copy in reversed(square_copies):
         copy.start()
     total = square[...]
     for step in range(1, n_ch):

time: 11.2 us -> 11.5 us (1.027)
  the two profiles are of different devices: /device:TPU:4 before, /device:TPU:0 now
where the time goes in v3:
time: 11.5 us; the launch traced here: 11.3 us
  Pallas kernels  10.7 us (93%)
  local copies, waits for them, and re-layouts  0.62 us (5%)
    pallas_call x1, Pallas kernels, body(): pl.pallas_call(functools.partial(kernel, n_ctx, n_ch), out_shape=pltpu.VM...  10.7 us
    unnamed x1, local copies, waits for them, and re-layouts  0.62 us

profile of v3, /device:TPU:0, one launch (start us, length us, event | category | flops | bytes accessed | tf_op | source)
XLA Modules:
  0.0 11.3 jit_solution(4642709624617841826)
XLA Ops:
  0.0 10.7 %shard_map.73 = bf16[16,1024]{1,0:T(8,128)(2,1)S(1)} custom-call(bf16[16,1024]{1,0:T(8,128)(2,1)} %query_hbm.1, bf16[16,1024]{1,0:T(8,128)(2,1)} %key_hbm.1, bf16[16,1024]{1,0:T(8,128)(2,1)} %value_hbm.1, f32[16,16]{1,0:T(8,128)} %residue_hbm.1, f32[16,16]{1,0:T(8,128)} %rate_hbm.1, f32[1,16]{1,0:T(1,128)} %bitcast.2, f32[1,16]{1,0:T(1,128)} %bitcast.3), custom_call_target="tpu_custom_call" | custom-call | flops 150000000 | bytes 140000 | tf_op jit(solution)/shard_map/pallas_call | solution.py:210
  10.7 0.6 %copy.9 = bf16[16,1024]{1,0:T(8,128)(2,1)} copy(bf16[16,1024]{1,0:T(8,128)(2,1)S(1)} %shard_map.73) | data formatting | bytes 65536
